TPU v7x, 32 devices: a whole 2x2x4 slice. The times are simulated.
32 devices in a mesh: blk: 8 (over y, x, core), grp: 4 (over z).
Axes of the slice: x: 2, y: 2, z: 4, core: 2. Of those that a mesh axis runs over, the one named last changes fastest.
Arguments:
- source_emb: float32 [8, 512, 400], P('blk', 'grp'), may hold values from -1.2 to 1.2
- source_state: float32 [8, 512], P('blk', 'grp'), may hold values from 0.01 to 0.1
- target_emb: float32 [8, 512, 400], P('blk', 'grp'), may hold values from -1.2 to 1.2
- target_state: float32 [8, 512], P('blk', 'grp'), may hold values from 0.01 to 0.1
- relation_emb: float32 [512, 400], replicated, may hold values from 0.1 to 1.9
- relation_state: float32 [512], replicated, may hold values from 0.01 to 0.1
- source_ids: int32 [2, 8, 4, 512], P(None, 'blk', 'grp'), may hold values from 0 to 127
- target_ids: int32 [2, 8, 4, 512], P(None, 'blk', 'grp'), may hold values from 0 to 127
- relation_ids: int32 [2, 8, 4, 512], P(None, 'blk', 'grp'), may hold values from 0 to 511
- edge_counts: int32 [2, 8, 4], P(None, 'blk', 'grp'), may hold values from 128 to 512, as said below
- sample_ids: int32 [2, 8, 4, 1, 256], P(None, 'blk', 'grp'), may hold values from 0 to 127
Outputs:
- source_out: float32 [8, 512, 400], P('blk', 'grp')
- source_state_out: float32 [8, 512], P('blk', 'grp')
- target_out: float32 [8, 512, 400], P('blk', 'grp')
- target_state_out: float32 [8, 512], P('blk', 'grp')
- relation_out: float32 [512, 400], replicated
- relation_state_out: float32 [512], replicated
Inputs may be any that keep to these rules, and one draw needn't show every extreme that they name: `edge_counts`: in every round some bucket is full.
All inputs are finite; a program needn't handle non-finite values.
Results may differ from a plain program's by a relative error of at most 0.0003.
Values sent between devices are 32-bit elements; how exact they have to be, the bound alone decides.
A program may use at most 64 MiB of HBM per device.

v0:
```python
import jax
import jax.numpy as jnp
from jax import lax
from jax.sharding import PartitionSpec as P

learning_rate = 0.1
relation_rate = 0.1


def passed_along(block, axis, distance):
    devices = range(lax.axis_size(axis))
    route = [((i - distance) % len(devices), i) for i in devices]
    return lax.ppermute(block, axis, route)


def adagrad(weights, accum, grads, rate):
    fresh = accum + jnp.mean(grads * grads, axis=-1)
    return (weights - rate * grads * lax.rsqrt(fresh)[..., None], fresh)


def pick_rows(selector, table):
    return jnp.dot(selector, table, precision=lax.Precision.HIGHEST)


def put_rows(selector, values):
    return jnp.einsum("ir,id->rd", selector, values, precision=lax.Precision.HIGHEST)


def on_device(
    source_emb,
    source_state,
    target_emb,
    target_state,
    relation_emb,
    relation_state,
    source_ids,
    target_ids,
    relation_ids,
    edge_counts,
    sample_ids,
):
    source_rows = source_emb[0]
    source_acc = source_state[0]
    target_rows = target_emb[0]
    target_acc = target_state[0]
    rounds = source_ids.shape[0]
    slots = source_ids.shape[3]
    blocks = sample_ids.shape[3]
    samples = sample_ids.shape[4]
    per_block = slots // blocks
    slab_rows = source_rows.shape[0]
    kinds = relation_emb.shape[0]
    row_iota = jnp.arange(slab_rows, dtype=jnp.int32)
    total = jnp.zeros(relation_emb.shape, jnp.float32)
    for round_index in range(rounds):
        these_source = source_ids[round_index, 0, 0]
        these_target = target_ids[round_index, 0, 0]
        these_kinds = relation_ids[round_index, 0, 0]
        these_samples = sample_ids[round_index, 0, 0]
        live_count = edge_counts[round_index, 0, 0]
        held_source = source_rows
        held_target = target_rows

        def visit(block_index, running):
            grad_source, grad_target, grad_relation = running
            first = block_index * per_block
            picked_samples = lax.dynamic_index_in_dim(these_samples, block_index, 0, keepdims=False)
            alive = (first + jnp.arange(per_block, dtype=jnp.int32) < live_count).astype(
                jnp.float32
            )
            source_hot = (these_source[:, None] == row_iota[None, :]).astype(jnp.float32)
            target_hot = (these_target[:, None] == row_iota[None, :]).astype(jnp.float32)
            sample_hot = (picked_samples[:, None] == row_iota[None, :]).astype(jnp.float32)
            scale = relation_emb[these_kinds]
            left = pick_rows(source_hot, held_source)
            right = pick_rows(target_hot, held_target)
            sampled = pick_rows(sample_hot, held_target)
            query = left * scale
            positive = jnp.sum(query * right, axis=-1)
            negative = jnp.einsum("id,jd->ij", query, sampled, precision=lax.Precision.HIGHEST)
            pull = -alive * jax.nn.sigmoid(-positive)
            push = alive[:, None] * jax.nn.sigmoid(negative) / samples
            grad_query = pull[:, None] * right + jnp.dot(
                push, sampled, precision=lax.Precision.HIGHEST
            )
            grad_source = grad_source + put_rows(source_hot, grad_query * scale)
            to_samples = jnp.einsum("ij,id->jd", push, query, precision=lax.Precision.HIGHEST)
            grad_target = (
                grad_target
                + put_rows(target_hot, pull[:, None] * query)
                + put_rows(sample_hot, to_samples)
            )
            grad_relation = grad_relation + jax.ops.segment_sum(
                grad_query * left, these_kinds, num_segments=kinds
            )
            return (grad_source, grad_target, grad_relation)

        initial = (
            jnp.zeros_like(source_rows),
            jnp.zeros_like(target_rows),
            jnp.zeros(relation_emb.shape, jnp.float32),
        )
        grad_source, grad_target, grad_relation = lax.fori_loop(0, blocks, visit, initial)
        total = total + lax.psum(grad_relation, ("blk", "grp"))
        target_rows, target_acc = adagrad(target_rows, target_acc, grad_target, learning_rate)
        source_rows, source_acc = adagrad(source_rows, source_acc, grad_source, learning_rate)
        if round_index + 1 < rounds:
            source_rows, source_acc = passed_along((source_rows, source_acc), "blk", 1)
    relation_out, relation_state_out = adagrad(relation_emb, relation_state, total, relation_rate)
    return (
        source_rows[None],
        source_acc[None],
        target_rows[None],
        target_acc[None],
        relation_out,
        relation_state_out,
    )


def solution(mesh):
    in_specs = (
        P("blk", "grp", None),
        P("blk", "grp"),
        P("blk", "grp", None),
        P("blk", "grp"),
        P(),
        P(),
        P(None, "blk", "grp", None),
        P(None, "blk", "grp", None),
        P(None, "blk", "grp", None),
        P(None, "blk", "grp"),
        P(None, "blk", "grp", None, None),
    )
    out_specs = (
        P("blk", "grp", None),
        P("blk", "grp"),
        P("blk", "grp", None),
        P("blk", "grp"),
        P(),
        P(),
    )
    return jax.shard_map(
        on_device, mesh=mesh, in_specs=in_specs, out_specs=out_specs, check_vma=False
    )
```

profile of v0, /device:TPU:1, one launch (start us, length us, event | category | flops | bytes accessed | tf_op | source)
XLA Modules:
  0.0 200.1 jit_solution(17178408586867470361)
XLA Ops:
  7.2 0.0 all-reduce.2.cloned.1.call-start
  7.2 0.7 fusion.49
  7.9 1.5 copy.23
  9.4 0.0 copy-done.6
  9.4 1.6 gather_fusion
  11.1 0.0 copy-start.7
  11.1 0.0 copy-start.4
  11.1 0.3 copy.24
  11.4 0.4 copy-done.7
  11.8 0.7 copy-done.8
  12.5 0.7 copy-done.9
  13.1 0.6 fusion.52
  13.7 0.6 fusion.45
  14.4 0.0 copy-start.2
  14.4 0.6 fusion.27
  15.0 0.3 copy-done.2
  15.3 0.4 fusion.28
  15.7 0.7 multiply_reduce_fusion.2
  16.4 0.7 divide_multiply_fusion.1
  17.0 1.9 fusion.8
  18.9 1.8 fusion.53
  20.7 0.6 multiply_reduce_fusion.6
  21.4 0.7 copy-done.12
  22.0 0.5 rsqrt_multiply_fusion.4
  22.5 0.7 bitcast_subtract_fusion.1
  23.2 2.6 %collective-permute-start = (f32[128,400]{0,1:T(8,128)}, f32[128,400]{0,1:T(8,128)}, u32[]{:S(2)}, u32[]{:S(2)}) collective-permute-start(f32[128,400]{0,1:T(8,128)} %bitcast_subtract_fusion.1), channel_id=1, source_target_pairs={{28,0},{0,4},{4,8},{8,12},{12,16},{16,20},{20,24},{24,28},{29,1},{... | collective-permute-start | bytes 614408 | tf_op jit(solution)/shard_map/ppermute | solution.py:13
  25.8 0.0 collective-permute-start.1
  25.9 1.3 fusion.14
  27.2 1.8 fusion.55
  29.0 1.6 gather_fusion.1
  30.6 0.3 copy.27
  30.9 0.7 fusion.46
  31.6 0.0 copy-start.5
  31.6 2.5 %copy.29 = f32[512,400]{1,0:T(8,128)} copy(f32[512,400]{0,1:T(8,128)} %get-tuple-element.134) | data formatting | bytes 1638400 | tf_op jit(solution)/shard_map/while/body/eval_jaxpr/mul | solution.py:94
  34.1 0.6 multiply_reduce_fusion.5
  34.7 0.7 copy-done.11
  35.4 0.0 copy-done.3
  35.4 4.7 %scatter_custom_fusion = f32[512,400]{1,0:T(8,128)S(1)} fusion(s32[512]{0:T(512)S(1)} %bitcast.81, f32[512,400]{1,0:T(8,128)} %copy.29, f32[]{:T(128)} %constant.39.clone.1), kind=kCustom, calls=%fused_computation.34 | custom fusion | flops 204800 | bytes 819712 | tf_op jit(solution)/shard_map/while/body/eval_jaxpr/scatter-add | solution.py:93
  40.2 0.4 fusion.32
  40.6 0.0 collective-permute-done
  40.6 1.5 fusion.25
  42.1 0.7 multiply_reduce_fusion.1
  42.8 0.7 divide_multiply_fusion
  43.5 0.6 fusion.10
  44.1 1.9 fusion.9
  46.0 1.8 fusion.56
  47.8 1.8 fusion.54
  49.6 0.6 multiply_reduce_fusion.4
  50.2 0.6 multiply_reduce_fusion.3
  50.9 0.5 copy-done.1
  51.4 1.3 copy.30
  52.7 5.3 %scatter_custom_fusion.1 = f32[512,400]{1,0:T(8,128)} fusion(s32[512]{0:T(512)S(1)} %bitcast.80, f32[512,400]{1,0:T(8,128)} %copy.30, f32[]{:T(128)} %constant.39.clone.1), kind=kCustom, calls=%fused_computation.32 | custom fusion | flops 204800 | bytes 819712 | tf_op jit(solution)/shard_map/while/body/eval_jaxpr/scatter-add | solution.py:93
  58.0 2.5 %add.156 = f32[512,400]{1,0:T(8,128)} add(f32[512,400]{1,0:T(8,128)S(1)} %scatter_custom_fusion, f32[512,400]{1,0:T(8,128)} %scatter_custom_fusion.1) | non-fusion elementwise | flops 204800 | bytes 2457600 | tf_op jit(solution)/shard_map/add | solution.py:104
  60.4 0.0 all-reduce.2.cloned.1.call-update
  60.5 0.7 subtract_bitcast_fusion
  61.2 0.5 bitcast_add_fusion
  61.7 0.0 collective-permute-done.1
  61.7 1.1 fusion.47
  62.8 1.6 subtract_bitcast_fusion.1
  64.4 125.3 %all-reduce.2.cloned.1.call-done = f32[512,400]{1,0:T(8,128)} async-done(((f32[512,400]{1,0:T(8,128)}), f32[512,400]{1,0:T(8,128)}) %all-reduce.2.cloned.1.call-update) | async-done | bytes 819216 | tf_op jit(solution)/shard_map/psum | solution.py:104
  189.8 1.5 multiply_reduce_fusion
  191.2 0.6 rsqrt_multiply_fusion
  191.8 0.2 multiply_subtract_fusion
  192.0 1.2 copy.32
  (22 shorter events, 0.1 us)
Async XLA Ops:
  7.2 182.6 %all-reduce.2.cloned.1.call-start = ((), (), s32[]{:S(2)}) async-start(), calls=%async_computation | async-start | bytes 2097152 | tf_op jit(solution)/shard_map/psum | solution.py:104
  7.9 1.5 copy-start.6
  11.1 0.7 copy-start.7
  11.1 3.3 %copy-start.4 = (f32[1,128,400]{1,2,0:T(8,128)S(1)}, f32[1,128,400]{1,2,0:T(8,128)}, u32[]{:S(2)}) copy-start(f32[1,128,400]{1,2,0:T(8,128)} %param.11) | copy-start | bytes 614404
  11.8 0.7 copy-start.8
  12.4 0.7 copy-start.9
  14.4 0.9 copy-start.2
  21.4 0.7 copy-start.12
  23.2 17.4 %collective-permute-start = (f32[128,400]{0,1:T(8,128)}, f32[128,400]{0,1:T(8,128)}, u32[]{:S(2)}, u32[]{:S(2)}) collective-permute-start(f32[128,400]{0,1:T(8,128)} %bitcast_subtract_fusion.1), channel_id=1, source_target_pairs={{28,0},{0,4},{4,8},{8,12},{12,16},{16,20},{20,24},{24,28},{29,1},{... | collective-permute-start | bytes 614408 | tf_op jit(solution)/shard_map/ppermute | solution.py:13
  25.8 35.9 %collective-permute-start.1 = (f32[128]{0:T(128)}, f32[128]{0:T(128)}, u32[]{:S(2)}, u32[]{:S(2)}) collective-permute-start(f32[128]{0:T(128)} %get-tuple-element.92), channel_id=1, source_target_pairs={{28,0},{0,4},{4,8},{8,12},{12,16},{16,20},{20,24},{24,28},{29,1},{... | collective-permute-start | bytes 1544 | tf_op jit(solution)/shard_map/ppermute | solution.py:13
  31.6 2.5 %copy-start.5 = (f32[128,400]{0,1:T(8,128)S(1)}, f32[128,400]{0,1:T(8,128)}, u32[]{:S(2)}) copy-start(f32[128,400]{0,1:T(8,128)} %fusion.14) | copy-start | bytes 614404
  34.1 1.3 copy-start.3
  34.7 0.7 copy-start.11
  50.2 1.1 copy-start.1
  64.4 126.8 %copy-start.10 = (f32[512]{0:T(512)S(1)}, f32[512]{0:T(512)}, u32[]{:S(2)}) copy-start(f32[512]{0:T(512)} %param.16) | copy-start | bytes 6148
  189.8 2.1 %copy-start = (f32[512,400]{1,0:T(8,128)S(1)}, f32[512,400]{1,0:T(8,128)}, u32[]{:S(2)}) copy-start(f32[512,400]{1,0:T(8,128)} %all-reduce.2.cloned.1.call-done) | copy-start | bytes 2457604
Sparse Core Ops, SparseCore 0:
  60.6 129.1 all-reduce.1
where the time goes:
time: 202 us; the launch traced here: 200 us
  waiting for transfers between devices  125 us (62%)
  other arithmetic  22.6 us (11%)
  matrix products  19.7 us (10%)
  local copies, waits for them, and re-layouts  15.5 us (8%)
  between operations  14.3 us (7%)
  starting transfers between devices  2.66 us (1%)
    psum x1, waiting for transfers between devices, on_device(): total = total + lax.psum(grad_relation, ('blk', 'grp'))  125 us
    scatter-add x2, other arithmetic, visit(): jax.ops.segment_sum(grad_query * left, these_kinds, num_segments=kinds)  10 us
    unnamed x28, local copies, waits for them, and re-layouts  6.54 us
    dot_general x6, matrix products, put_rows(): jnp.einsum('ir,id->rd', selector, values, precision=lax.Precision.HIGHEST)  4.43 us
    dot_general x6, matrix products, pick_rows(): return jnp.dot(selector, table, precision=lax.Precision.HIGHEST)  4.27 us
  transfers between devices with their start and end apart: 3, of which 1 were waited for; matrix products, arithmetic and copies ran while one was open for 19% of the time, Pallas kernels for 0%

commit v1 on v0

v1 whole, which is shorter than its diff:
```python
import functools

import jax
import jax.numpy as jnp
from jax import lax
from jax.experimental import pallas as pl
from jax.experimental.pallas import tpu as pltpu
from jax.sharding import PartitionSpec as P

RATE = 0.1
SUBLANES = 8
MESH = pl.DeviceIdType.MESH
BF16 = jnp.bfloat16
F32 = jnp.float32


def halves_of(x):
    high = x.astype(BF16)
    return high, (x - high.astype(F32)).astype(BF16)


def mm(a, b):
    return jnp.dot(a, b, preferred_element_type=F32)


def mm_nt(a, b):
    return lax.dot_general(a, b, (((1,), (1,)), ((), ())), preferred_element_type=F32)


def adagrad(weights, sums, grads):
    fresh = sums + jnp.sum(grads * grads, axis=0, keepdims=True) * (1.0 / grads.shape[0])
    return weights - RATE * grads * lax.rsqrt(fresh), fresh


def plan(n, m, width):
    steps = []
    tiles = width // SUBLANES
    for _ in range(1, n.bit_length() - 1):
        each, both = tiles // 2, tiles % 2
        steps.append((each, both))
        tiles = each + both
    return steps, (tiles // m, tiles % m)


def copy_count(n, m, width, rounds):
    steps, (each, both) = plan(n, m, width)
    out = 2 * sum(1 for step in steps if step[0]) + 2 * (m - 1) * (each > 0)
    back = 2 * (m - 1) * ((each > 0) + (both > 0))
    return (rounds - 1) + 2 + 2 * len(steps) + back + out + 2


def kernel(
    n,
    m,
    source_ref,
    source_state_ref,
    target_ref,
    target_state_ref,
    relation_ref,
    relation_state_ref,
    source_ids_ref,
    target_ids_ref,
    relation_ids_ref,
    counts_ref,
    samples_ref,
    source_out,
    source_state_out,
    target_out,
    target_state_out,
    relation_out,
    relation_state_out,
    hot_ref,
    grads,
    result,
    slab_send,
    slab_recv,
    first_recv,
    step_recv,
    grp_recv,
    send_sem,
    recv_sem,
):
    blk, grp = lax.axis_index("blk"), lax.axis_index("grp")
    bits = n.bit_length() - 1
    rounds = source_ids_ref.shape[0]
    slots = source_ids_ref.shape[3]
    samples = samples_ref.shape[4]
    width, rows = source_ref.shape[1:]
    kinds = relation_ref.shape[1]
    quarter = kinds // 4
    steps, (grp_each, grp_both) = plan(n, m, width)
    after, before = lax.rem(blk + 1, n), lax.rem(blk + n - 1, n)

    def bit_of(bit):
        return lax.rem(blk // (1 << bit), 2)

    def flipped(bit):
        return blk + (1 << bit) - 2 * (1 << bit) * bit_of(bit)

    barrier = pltpu.get_barrier_semaphore()
    greeted = [(after, grp), (before, grp)]
    greeted += [(flipped(bit), grp) for bit in range(bits)]
    greeted += [(blk, lax.rem(grp + step, m)) for step in range(1, m)]
    for where in greeted:
        pl.semaphore_signal(barrier, inc=1, device_id=where, device_id_type=MESH)

    started, sent = [], []

    def send(src, dst, where):
        copy = pltpu.make_async_remote_copy(
            src_ref=src,
            dst_ref=dst,
            send_sem=send_sem.at[len(started)],
            recv_sem=recv_sem.at[len(started)],
            device_id=where,
            device_id_type=MESH,
        )
        copy.start()
        started.append(copy)
        return copy

    table_high, table_low = halves_of(relation_ref[...])

    def relation_side(index):
        picked = relation_ids_ref[index, 0]
        hot = (lax.broadcasted_iota(jnp.int32, (kinds, slots), 0) == picked).astype(BF16)
        hot_ref[index] = hot
        return mm(table_high, hot) + mm(table_low, hot)

    def edge_side(index):
        row_iota = lax.broadcasted_iota(jnp.int32, (rows, slots), 0)
        source_hot = (row_iota == source_ids_ref[index, 0]).astype(BF16)
        target_hot = row_iota == target_ids_ref[index, 0]
        sample_iota = lax.broadcasted_iota(jnp.int32, (rows, samples), 0)
        named = (sample_iota == samples_ref[index, 0, 0]).astype(F32)
        share = jnp.sum(named, axis=1, keepdims=True) * (1.0 / samples)
        alive = (
            lax.broadcasted_iota(jnp.int32, (1, slots), 1) < counts_ref[0, 0, index]
        ).astype(F32)
        return source_hot, target_hot, share, alive

    source, source_sums = source_ref[0], source_state_ref[...]
    target, target_sums = target_ref[0], target_state_ref[...]
    scale = relation_side(0)
    edges = edge_side(0)
    pl.semaphore_wait(barrier, len(greeted))

    for index in range(rounds):
        source_hot, target_hot, share, alive = edges
        source_high, source_low = halves_of(source)
        left = mm(source_high, source_hot) + mm(source_low, source_hot)
        query = left * scale
        query_high, query_low = halves_of(query)
        flat_high, flat_low = halves_of(target.T)
        logits = mm(flat_high, query_high) + (
            mm(flat_low, query_high) + mm(flat_high, query_low)
        )
        positive = jnp.sum(jnp.where(target_hot, logits, 0.0), axis=0, keepdims=True)
        pull = -alive * jax.nn.sigmoid(-positive)
        push = share * alive * jax.nn.sigmoid(logits)
        weight = jnp.where(target_hot, pull, 0.0) + push
        weight_high, weight_low = halves_of(weight)
        target_high, target_low = halves_of(target)
        grad_query = mm(target_high, weight_high) + (
            mm(target_low, weight_high) + mm(target_high, weight_low)
        )

        def source_step():
            high, low = halves_of(grad_query * scale)
            fresh = mm_nt(high, source_hot) + mm_nt(low, source_hot)
            return adagrad(source, source_sums, fresh)

        def target_step():
            fresh = mm_nt(query_high, weight_high) + (
                mm_nt(query_high, weight_low) + mm_nt(query_low, weight_high)
            )
            return adagrad(target, target_sums, fresh)

        def relation_part(core):
            high, low = halves_of(grad_query * left)
            hot = hot_ref[index, pl.ds(pl.multiple_of(core * 2 * quarter, quarter), 2 * quarter)]
            fresh = mm_nt(high, hot) + mm_nt(low, hot)
            for part in range(2):
                piece = fresh[:, part * quarter : (part + 1) * quarter]
                if index == 0:
                    grads[core, part] = piece
                else:
                    grads[core, part] += piece

        if index + 1 < rounds:
            new_source, new_sums = source_step()
            slab_send[index, :width] = new_source
            slab_send[index, width:] = jnp.broadcast_to(new_sums, (SUBLANES, rows))
            copy = send(slab_send.at[index], slab_recv.at[index], (after, grp))
            new_target, new_target_sums = target_step()
            relation_part(0)
            relation_part(1)
            scale = relation_side(index + 1)
            edges = edge_side(index + 1)
            target, target_sums = new_target, new_target_sums
            copy.wait_recv()
            source = slab_recv[index, :width]
            source_sums = slab_recv[index, width : width + 1]

    mine = bit_of(0)
    core = (flipped(0), grp)
    relation_part(1 - mine)
    first_copies = [
        send(grads.at[1 - mine, part], first_recv.at[part], core) for part in range(2)
    ]
    relation_part(mine)
    new_source, new_sums = source_step()
    source_out[0] = new_source
    source_state_out[...] = new_sums

    orders = [list(range(1, bits)), list(range(bits - 1, 0, -1))]
    bases = [0, 0]
    history = [[], []]
    pending = [None, None]
    grp_copies = [[], []]

    def span(base, tiles):
        return pl.ds(pl.multiple_of(base * SUBLANES, SUBLANES), tiles * SUBLANES)

    def piece(part, base, tiles):
        return grads.at[mine, part, span(base, tiles)]

    def launch(part, step):
        each, both = steps[step]
        bit = orders[part][step]
        high = bit_of(bit)
        base = bases[part]
        where = (flipped(bit), grp)
        pending[part] = send(
            piece(part, base + (1 - high) * each, each + both),
            step_recv.at[part, step, pl.ds(0, (each + both) * SUBLANES)],
            where,
        )
        history[part].append((where, base, base + high * (each + both), each))
        bases[part] = base + high * each

    def launch_grp(part):
        base = bases[part]
        for step in range(1, m):
            peer = lax.rem(grp + step, m)
            if grp_each:
                copy = send(
                    piece(part, base + peer * grp_each, grp_each),
                    grp_recv.at[part, step - 1, pl.ds(0, grp_each * SUBLANES)],
                    (blk, peer),
                )
                grp_copies[part].append(copy)
            if grp_both:
                copy = send(
                    piece(part, base + m * grp_each, grp_both),
                    grp_recv.at[
                        part, step - 1, pl.ds(grp_each * SUBLANES, grp_both * SUBLANES)
                    ],
                    (blk, peer),
                )
                grp_copies[part].append(copy)

    def advance(part, step):
        if step < len(steps):
            launch(part, step)
        else:
            launch_grp(part)

    for part in range(2):
        first_copies[part].wait_recv()
        grads[mine, part] += first_recv[part]
        advance(part, 0)
    new_target, new_target_sums = target_step()
    target_out[0] = new_target
    target_state_out[...] = new_target_sums
    for step in range(len(steps)):
        each, both = steps[step]
        for part in range(2):
            pending[part].wait_recv()
            if both:
                pending[part].wait_send()
                sent.append(id(pending[part]))
            where = span(bases[part], each + both)
            grads[mine, part, where] += step_recv[part, step, : (each + both) * SUBLANES]
            advance(part, step + 1)

    def summed(part, base, first, tiles):
        own = grads[mine, part, span(base, tiles)]
        total = None
        for member in range(m):
            slot = lax.max(lax.rem(grp - member + m, m) - 1, 0)
            came = grp_recv[part, slot, first * SUBLANES : (first + tiles) * SUBLANES]
            term = jnp.where(grp == member, own, came)
            total = term if total is None else total + term
        result[mine, part, span(base, tiles)] = total

    out_pending = [[], []]
    for part in range(2):
        for copy in grp_copies[part]:
            copy.wait_recv()
        base = bases[part]
        if grp_both:
            summed(part, base + m * grp_each, grp_each, grp_both)
        if grp_each:
            summed(part, base + grp * grp_each, 0, grp_each)
            for step in range(1, m):
                ref = result.at[mine, part, span(base + grp * grp_each, grp_each)]
                out_pending[part].append(send(ref, ref, (blk, lax.rem(grp + step, m))))
    for back in range(len(steps) - 1, -1, -1):
        for part in range(2):
            where, base, first, each = history[part][back]
            for copy in out_pending[part]:
                copy.wait_recv()
            out_pending[part] = []
            if each:
                ref = result.at[mine, part, span(first, each)]
                out_pending[part] = [send(ref, ref, where)]
    for part in range(2):
        for copy in out_pending[part]:
            copy.wait_recv()
        ref = result.at[mine, part]
        out_pending[part] = [send(ref, ref, core)]
    for part in range(2):
        out_pending[part][0].wait_recv()
    for side in range(2):
        for part in range(2):
            lanes = slice((2 * side + part) * quarter, (2 * side + part + 1) * quarter)
            fresh, sums = adagrad(
                relation_ref[:, lanes], relation_state_ref[:, lanes], result[side, part]
            )
            relation_out[:, lanes] = fresh
            relation_state_out[:, lanes] = sums
    for copy in started:
        if id(copy) not in sent:
            copy.wait_send()


def on_device(n, m, *arrays):
    arrays = list(arrays)
    rounds, slots = arrays[6].shape[0], arrays[6].shape[3]
    kinds, width = arrays[4].shape
    rows = arrays[0].shape[1]
    arrays[0] = jnp.swapaxes(arrays[0], 1, 2)
    arrays[2] = jnp.swapaxes(arrays[2], 1, 2)
    arrays[4] = arrays[4].T
    arrays[5] = arrays[5].reshape(1, kinds)
    arrays[9] = jnp.transpose(arrays[9], (1, 2, 0))
    quarter = kinds // 4
    steps, (grp_each, grp_both) = plan(n, m, width)
    copies = copy_count(n, m, width, rounds)
    largest = SUBLANES * sum(steps[0])
    slab = (max(rounds - 1, 1), width + SUBLANES, rows)
    vmem = pl.BlockSpec(memory_space=pltpu.VMEM)
    smem = pl.BlockSpec(memory_space=pltpu.SMEM)
    outs = pl.pallas_call(
        functools.partial(kernel, n, m),
        out_shape=[jax.ShapeDtypeStruct(a.shape, F32) for a in arrays[:6]],
        in_specs=[vmem] * 9 + [smem, vmem],
        out_specs=[vmem] * 6,
        scratch_shapes=[
            pltpu.VMEM((rounds, kinds, slots), BF16),
            pltpu.VMEM((2, 2, width, quarter), F32),
            pltpu.VMEM((2, 2, width, quarter), F32),
            pltpu.VMEM(slab, F32),
            pltpu.VMEM(slab, F32),
            pltpu.VMEM((2, width, quarter), F32),
            pltpu.VMEM((2, len(steps), largest, quarter), F32),
            pltpu.VMEM((2, m - 1, (grp_each + grp_both) * SUBLANES, quarter), F32),
            pltpu.SemaphoreType.DMA((copies,)),
            pltpu.SemaphoreType.DMA((copies,)),
        ],
        compiler_params=pltpu.CompilerParams(
            collective_id=0, has_side_effects=True, vmem_limit_bytes=40 * 2**20
        ),
        name="train",
    )(*arrays)
    return (
        jnp.swapaxes(outs[0], 1, 2),
        outs[1],
        jnp.swapaxes(outs[2], 1, 2),
        outs[3],
        outs[4].T,
        outs[5].reshape(kinds),
    )


def solution(mesh):
    n, m = mesh.shape["blk"], mesh.shape["grp"]
    in_specs = (
        P("blk", "grp", None),
        P("blk", "grp"),
        P("blk", "grp", None),
        P("blk", "grp"),
        P(),
        P(),
        P(None, "blk", "grp", None),
        P(None, "blk", "grp", None),
        P(None, "blk", "grp", None),
        P(None, "blk", "grp"),
        P(None, "blk", "grp", None, None),
    )
    out_specs = (
        P("blk", "grp", None),
        P("blk", "grp"),
        P("blk", "grp", None),
        P("blk", "grp"),
        P(),
        P(),
    )
    return jax.shard_map(
        functools.partial(on_device, n, m),
        mesh=mesh,
        in_specs=in_specs,
        out_specs=out_specs,
        check_vma=False,
    )
```

time: 202 us -> 51.1 us (0.25)
  waiting for transfers between devices: 125 us -> 0 us
  Pallas kernels: 0 us -> 39.9 us
  other arithmetic: 22.6 us -> 0 us
  matrix products: 19.7 us -> 0 us
  between operations: 14.3 us -> 0.69 us
  local copies, waits for them, and re-layouts: 15.5 us -> 10.2 us
  starting transfers between devices: 2.66 us -> 0 us
    psum x1 -> x0, waiting for transfers between devices: 125 us -> none  [on_device(): total = total + lax.psum(grad_relation, ('blk', 'grp'))]
    pallas_call x0 -> x1, Pallas kernels: none -> 39.9 us  [on_device(): pl.pallas_call(functools.partial(kernel, n, m), out_shape=[jax.ShapeDtype...]
    dot_general x18 -> x0, matrix products: 19.7 us -> none  [the longest x6 4.43 us: put_rows(): jnp.einsum('ir,id->rd', selector, values, precision=lax.Precision.HIGHEST)]
    scatter-add x2 -> x0, other arithmetic: 10 us -> none  [visit(): jax.ops.segment_sum(grad_query * left, these_kinds, num_segments=kinds)]
    gather x4 -> x0, local copies, waits for them, and re-layouts: 3.84 us -> none  [visit(): scale = relation_emb[these_kinds]]
    mul x2 -> x0, local copies, waits for them, and re-layouts: 3.81 us -> none  [visit(): grad_query * left]
    unnamed x28, local copies, waits for them, and re-layouts: 6.54 us -> 10.2 us
    broadcast_in_dim x3 -> x0, other arithmetic: 3.46 us -> none  [the longest x1 1.64 us: on_device(): source_rows[None]]
  transfers between devices with their start and end apart: 3 -> 0, of which waited for: 1 -> 0; matrix products, arithmetic and copies ran while one was open for 19% -> 0% of each run, Pallas kernels for 0% -> 0%
where the time goes in v1:
time: 51.1 us; the launch traced here: 50.8 us
  Pallas kernels  39.9 us (78%)
  local copies, waits for them, and re-layouts  10.2 us (20%)
  between operations  0.69 us (1%)
    pallas_call x1, Pallas kernels, on_device(): pl.pallas_call(functools.partial(kernel, n, m), out_shape=[jax.ShapeDtype...  39.9 us
    unnamed x28, local copies, waits for them, and re-layouts  10.2 us

profile of v1, /device:TPU:1, one launch (start us, length us, event | category | flops | bytes accessed | tf_op | source)
XLA Modules:
  0.0 50.8 jit_solution(13083991152169469500)
XLA Ops:
  0.6 0.0 copy-start.4
  0.6 0.0 copy-start.3
  0.7 0.0 copy-start.8
  0.7 0.0 copy-start.9
  0.7 0.6 %copy-done.4 = s32[2,1,1,512]{3,2,1,0:T(1,128)S(1)} copy-done((s32[2,1,1,512]{3,2,1,0:T(1,128)S(1)}, s32[2,1,1,512]{3,2,1,0:T(1,128)}, u32[]{:S(2)}) %copy-start.4) | copy-done | bytes 4120
  1.3 0.0 copy-done.3
  1.3 0.0 copy-done.8
  1.3 0.0 copy-done.9
  1.3 0.0 copy-start
  1.3 1.1 %copy-done = f32[512,400]{0,1:T(8,128)S(1)} copy-done((f32[512,400]{0,1:T(8,128)S(1)}, f32[512,400]{0,1:T(8,128)}, u32[]{:S(2)}) %copy-start) | copy-done | bytes 819224
  2.5 0.0 copy-start.1
  2.5 0.9 %copy-done.1 = f32[1,128,400]{1,2,0:T(8,128)S(1)} copy-done((f32[1,128,400]{1,2,0:T(8,128)S(1)}, f32[1,128,400]{1,2,0:T(8,128)}, u32[]{:S(2)}) %copy-start.1) | copy-done | bytes 204824
  3.4 0.0 copy-start.2
  3.4 0.9 %copy-done.2 = f32[1,128,400]{1,2,0:T(8,128)S(1)} copy-done((f32[1,128,400]{1,2,0:T(8,128)S(1)}, f32[1,128,400]{1,2,0:T(8,128)}, u32[]{:S(2)}) %copy-start.2) | copy-done | bytes 204824
  4.4 0.0 copy-start.5
  4.4 0.7 %copy-done.5 = s32[2,1,1,512]{3,2,1,0:T(1,128)S(1)} copy-done((s32[2,1,1,512]{3,2,1,0:T(1,128)S(1)}, s32[2,1,1,512]{3,2,1,0:T(1,128)}, u32[]{:S(2)}) %copy-start.5) | copy-done | bytes 4120
  5.0 0.0 copy-start.6
  5.0 0.7 %copy-done.6 = f32[512]{0:T(512)S(1)} copy-done((f32[512]{0:T(512)S(1)}, f32[512]{0:T(512)}, u32[]{:S(2)}) %copy-start.6) | copy-done | bytes 2072
  5.7 0.0 copy-start.7
  5.7 0.7 %copy-done.7 = s32[2,1,1,1,256]{4,3,2,1,0:T(1,128)S(1)} copy-done((s32[2,1,1,1,256]{4,3,2,1,0:T(1,128)S(1)}, s32[2,1,1,1,256]{4,3,2,1,0:T(1,128)}, u32[]{:S(2)}) %copy-start.7) | copy-done | bytes 2072
  6.4 0.0 copy-start.10
  6.4 0.7 %copy-done.10 = s32[2,1,1]{0,2,1:T(1,128)S(1)} copy-done((s32[2,1,1]{0,2,1:T(1,128)S(1)}, s32[2,1,1]{0,2,1:T(1,128)}, u32[]{:S(2)}) %copy-start.10) | copy-done | bytes 32
  7.1 39.9 %train.1 = (f32[1,400,128]{2,1,0:T(8,128)S(1)}, f32[1,128]{1,0:T(1,128)S(1)}, f32[1,400,128]{2,1,0:T(8,128)S(1)}, f32[1,128]{1,0:T(1,128)S(1)}, f32[400,512]{1,0:T(8,128)S(1)}, /*index=5*/f32[1,512]{1,0:T(1,128)S(1)}) custom-call(f32[1,400,128]{2,1,0:T(8,128)S(1)} %bitcast.13, f32[1,128]{1,0:T(1,128)S(1)} %copy-done.8, f32[1,400,128]{2,1,0:T(8,128)S(1)} %bitcast.14, ...), custom_call_target="tpu_custom_call" | custom-call | tf_op jit(solution)/shard_map/train/pallas_call | solution.py:355
  47.0 0.7 %copy.23 = f32[1,128,400]{1,2,0:T(8,128)} copy(f32[1,128,400]{1,2,0:T(8,128)S(1)} %bitcast.12) | data formatting | bytes 409600
  47.6 0.5 %copy.24 = f32[1,128]{1,0:T(1,128)} copy(f32[1,128]{1,0:T(1,128)S(1)} %get-tuple-element.25) | data formatting | bytes 1024
  48.2 0.7 %copy.25 = f32[1,128,400]{1,2,0:T(8,128)} copy(f32[1,128,400]{1,2,0:T(8,128)S(1)} %bitcast.11) | data formatting | bytes 409600
  48.8 0.5 %copy.26 = f32[1,128]{1,0:T(1,128)} copy(f32[1,128]{1,0:T(1,128)S(1)} %get-tuple-element.27) | data formatting | bytes 1024
  49.3 0.9 %copy.27 = f32[512,400]{0,1:T(8,128)} copy(f32[512,400]{0,1:T(8,128)S(1)} %bitcast.9) | data formatting | bytes 1638400
  50.2 0.6 %copy.28 = f32[512]{0:T(512)} copy(f32[512]{0:T(512)S(1)} %bitcast.16) | data formatting | bytes 4096
Async XLA Ops:
  0.6 0.7 %copy-start.4 = (s32[2,1,1,512]{3,2,1,0:T(1,128)S(1)}, s32[2,1,1,512]{3,2,1,0:T(1,128)}, u32[]{:S(2)}) copy-start(s32[2,1,1,512]{3,2,1,0:T(1,128)} %target_ids_ref.1) | copy-start | bytes 12292
  0.6 0.7 %copy-start.3 = (s32[2,1,1,512]{3,2,1,0:T(1,128)S(1)}, s32[2,1,1,512]{3,2,1,0:T(1,128)}, u32[]{:S(2)}) copy-start(s32[2,1,1,512]{3,2,1,0:T(1,128)} %source_ids_ref.1) | copy-start | bytes 12292
  0.7 0.7 %copy-start.8 = (f32[1,128]{1,0:T(1,128)S(1)}, f32[1,128]{1,0:T(1,128)}, u32[]{:S(2)}) copy-start(f32[1,128]{1,0:T(1,128)} %source_state_ref.1) | copy-start | bytes 1540
  0.7 0.7 %copy-start.9 = (f32[1,128]{1,0:T(1,128)S(1)}, f32[1,128]{1,0:T(1,128)}, u32[]{:S(2)}) copy-start(f32[1,128]{1,0:T(1,128)} %target_state_ref.1) | copy-start | bytes 1540
  1.3 1.1 %copy-start = (f32[512,400]{0,1:T(8,128)S(1)}, f32[512,400]{0,1:T(8,128)}, u32[]{:S(2)}) copy-start(f32[512,400]{0,1:T(8,128)} %param.15) | copy-start | bytes 2457604
  2.5 0.9 %copy-start.1 = (f32[1,128,400]{1,2,0:T(8,128)S(1)}, f32[1,128,400]{1,2,0:T(8,128)}, u32[]{:S(2)}) copy-start(f32[1,128,400]{1,2,0:T(8,128)} %param.11) | copy-start | bytes 614404
  3.4 0.9 %copy-start.2 = (f32[1,128,400]{1,2,0:T(8,128)S(1)}, f32[1,128,400]{1,2,0:T(8,128)}, u32[]{:S(2)}) copy-start(f32[1,128,400]{1,2,0:T(8,128)} %param.13) | copy-start | bytes 614404
  4.4 0.7 %copy-start.5 = (s32[2,1,1,512]{3,2,1,0:T(1,128)S(1)}, s32[2,1,1,512]{3,2,1,0:T(1,128)}, u32[]{:S(2)}) copy-start(s32[2,1,1,512]{3,2,1,0:T(1,128)} %relation_ids_ref.1) | copy-start | bytes 12292
  5.0 0.7 %copy-start.6 = (f32[512]{0:T(512)S(1)}, f32[512]{0:T(512)}, u32[]{:S(2)}) copy-start(f32[512]{0:T(512)} %param.16) | copy-start | bytes 6148
  5.7 0.7 %copy-start.7 = (s32[2,1,1,1,256]{4,3,2,1,0:T(1,128)S(1)}, s32[2,1,1,1,256]{4,3,2,1,0:T(1,128)}, u32[]{:S(2)}) copy-start(s32[2,1,1,1,256]{4,3,2,1,0:T(1,128)} %samples_ref.1) | copy-start | bytes 6148
  6.4 0.7 %copy-start.10 = (s32[2,1,1]{0,2,1:T(1,128)S(1)}, s32[2,1,1]{0,2,1:T(1,128)}, u32[]{:S(2)}) copy-start(s32[2,1,1]{0,2,1:T(1,128)} %param.20) | copy-start | bytes 28

commit v2 on v1

--- a/solution.py
+++ b/solution.py
@@ -12,6 +12,7 @@
 MESH = pl.DeviceIdType.MESH
 BF16 = jnp.bfloat16
 F32 = jnp.float32
+done = object()
 
 
 def halves_of(x):
@@ -32,9 +33,14 @@
     return weights - RATE * grads * lax.rsqrt(fresh), fresh
 
 
-def plan(n, m, width):
+def chunks_of(width):
+    tiles = width // SUBLANES
+    large = 1 << (tiles.bit_length() - 1)
+    return [(0, large), (large, tiles - large)] if large < tiles else [(0, tiles)]
+
+
+def plan(n, m, tiles):
     steps = []
-    tiles = width // SUBLANES
     for _ in range(1, n.bit_length() - 1):
         each, both = tiles // 2, tiles % 2
         steps.append((each, both))
@@ -43,15 +49,26 @@
 
 
 def copy_count(n, m, width, rounds):
-    steps, (each, both) = plan(n, m, width)
-    out = 2 * sum(1 for step in steps if step[0]) + 2 * (m - 1) * (each > 0)
-    back = 2 * (m - 1) * ((each > 0) + (both > 0))
-    return (rounds - 1) + 2 + 2 * len(steps) + back + out + 2
-
-
-def kernel(
+    count = rounds - 1
+    for _, tiles in chunks_of(width):
+        steps, (each, both) = plan(n, m, tiles)
+        unit = 2 + len(steps) + sum(1 for step in steps if step[0])
+        unit += (m - 1) * (2 * (each > 0) + (both > 0))
+        count += 2 * unit
+    return count
+
+
+def kernel(n, m, *refs):
+    hbm, refs = refs[:11], refs[11:]
+    outs, refs = refs[:6], refs[6:]
+    staged, refs = refs[:11], refs[11:]
+    inner(n, m, hbm, *staged, *outs, *refs)
+
+
+def inner(
     n,
     m,
+    hbm,
     source_ref,
     source_state_ref,
     target_ref,
@@ -79,7 +96,27 @@
     grp_recv,
     send_sem,
     recv_sem,
+    load_sem,
 ):
+    staged = (
+        source_ref,
+        source_state_ref,
+        target_ref,
+        target_state_ref,
+        relation_ref,
+        relation_state_ref,
+        source_ids_ref,
+        target_ids_ref,
+        relation_ids_ref,
+        counts_ref,
+        samples_ref,
+    )
+    loads = [
+        pltpu.make_async_copy(src, dst, load_sem.at[number])
+        for number, (src, dst) in enumerate(zip(hbm, staged))
+    ]
+    for number in (4, 8, 0, 6, 2, 7, 10, 9, 1, 3, 5):
+        loads[number].start()
     blk, grp = lax.axis_index("blk"), lax.axis_index("grp")
     bits = n.bit_length() - 1
     rounds = source_ids_ref.shape[0]
@@ -88,7 +125,6 @@
     width, rows = source_ref.shape[1:]
     kinds = relation_ref.shape[1]
     quarter = kinds // 4
-    steps, (grp_each, grp_both) = plan(n, m, width)
     after, before = lax.rem(blk + 1, n), lax.rem(blk + n - 1, n)
 
     def bit_of(bit):
@@ -119,6 +155,7 @@
         started.append(copy)
         return copy
 
+    loads[4].wait()
     table_high, table_low = halves_of(relation_ref[...])
 
     def relation_side(index):
@@ -139,9 +176,12 @@
         ).astype(F32)
         return source_hot, target_hot, share, alive
 
+    loads[8].wait()
+    scale = relation_side(0)
+    for number in (0, 6, 2, 7, 10, 9, 1, 3, 5):
+        loads[number].wait()
     source, source_sums = source_ref[0], source_state_ref[...]
     target, target_sums = target_ref[0], target_state_ref[...]
-    scale = relation_side(0)
     edges = edge_side(0)
     pl.semaphore_wait(barrier, len(greeted))
 
@@ -176,10 +216,11 @@
             )
             return adagrad(target, target_sums, fresh)
 
+        relation_high, relation_low = halves_of(grad_query * left)
+
         def relation_part(core):
-            high, low = halves_of(grad_query * left)
             hot = hot_ref[index, pl.ds(pl.multiple_of(core * 2 * quarter, quarter), 2 * quarter)]
-            fresh = mm_nt(high, hot) + mm_nt(low, hot)
+            fresh = mm_nt(relation_high, hot) + mm_nt(relation_low, hot)
             for part in range(2):
                 piece = fresh[:, part * quarter : (part + 1) * quarter]
                 if index == 0:
@@ -204,124 +245,114 @@
 
     mine = bit_of(0)
     core = (flipped(0), grp)
+    orders = [list(range(1, bits)), list(range(bits - 1, 0, -1))]
+
+    def span(base, tiles):
+        return pl.ds(pl.multiple_of(base * SUBLANES, SUBLANES), tiles * SUBLANES)
+
+    def summed(part, chunk, base, first, tiles):
+        own = grads[mine, part, span(base, tiles)]
+        total = None
+        for member in range(m):
+            slot = lax.max(lax.rem(grp - member + m, m) - 1, 0)
+            came = grp_recv[
+                chunk, part, slot, first * SUBLANES : (first + tiles) * SUBLANES
+            ]
+            term = jnp.where(grp == member, own, came)
+            total = term if total is None else total + term
+        result[mine, part, span(base, tiles)] = total
+
+    def reduce_unit(part, chunk, start, tiles):
+        steps, (grp_each, grp_both) = plan(n, m, tiles)
+        where = span(start, tiles)
+        copy = send(
+            grads.at[1 - mine, part, where], first_recv.at[part, where], core
+        )
+        yield
+        copy.wait_recv()
+        grads[mine, part, where] += first_recv[part, where]
+        base, history = start, []
+        for number, (each, both) in enumerate(steps):
+            bit = orders[part][number]
+            high = bit_of(bit)
+            partner = (flipped(bit), grp)
+            size = each + both
+            copy = send(
+                grads.at[mine, part, span(base + (1 - high) * each, size)],
+                step_recv.at[chunk, part, number, pl.ds(0, size * SUBLANES)],
+                partner,
+            )
+            history.append((partner, base + high * size, each))
+            base = base + high * each
+            yield
+            copy.wait_recv()
+            if both:
+                copy.wait_send()
+                sent.append(id(copy))
+            came = step_recv[chunk, part, number, : size * SUBLANES]
+            grads[mine, part, span(base, size)] += came
+        copies = []
+        for step in range(1, m):
+            peer = lax.rem(grp + step, m)
+            pieces = [(base + peer * grp_each, 0, grp_each)]
+            pieces += [(base + m * grp_each, grp_each, grp_both)]
+            for row, slot_row, count in pieces:
+                if count:
+                    landing = pl.ds(slot_row * SUBLANES, count * SUBLANES)
+                    copies.append(
+                        send(
+                            grads.at[mine, part, span(row, count)],
+                            grp_recv.at[chunk, part, step - 1, landing],
+                            (blk, peer),
+                        )
+                    )
+        yield
+        for copy in copies:
+            copy.wait_recv()
+        copies = []
+        if grp_each:
+            row = base + grp * grp_each
+            summed(part, chunk, row, 0, grp_each)
+            ref = result.at[mine, part, span(row, grp_each)]
+            for step in range(1, m):
+                copies.append(send(ref, ref, (blk, lax.rem(grp + step, m))))
+        if grp_both:
+            summed(part, chunk, base + m * grp_each, grp_each, grp_both)
+        yield
+        for partner, first, each in reversed(history):
+            for copy in copies:
+                copy.wait_recv()
+            copies = []
+            if each:
+                ref = result.at[mine, part, span(first, each)]
+                copies = [send(ref, ref, partner)]
+            yield
+        for copy in copies:
+            copy.wait_recv()
+        ref = result.at[mine, part, where]
+        copy = send(ref, ref, core)
+        yield
+        copy.wait_recv()
+
     relation_part(1 - mine)
-    first_copies = [
-        send(grads.at[1 - mine, part], first_recv.at[part], core) for part in range(2)
+    units = [
+        reduce_unit(part, chunk, start, tiles)
+        for chunk, (start, tiles) in enumerate(chunks_of(width))
+        for part in range(2)
     ]
+    for unit in units:
+        next(unit)
     relation_part(mine)
     new_source, new_sums = source_step()
     source_out[0] = new_source
     source_state_out[...] = new_sums
-
-    orders = [list(range(1, bits)), list(range(bits - 1, 0, -1))]
-    bases = [0, 0]
-    history = [[], []]
-    pending = [None, None]
-    grp_copies = [[], []]
-
-    def span(base, tiles):
-        return pl.ds(pl.multiple_of(base * SUBLANES, SUBLANES), tiles * SUBLANES)
-
-    def piece(part, base, tiles):
-        return grads.at[mine, part, span(base, tiles)]
-
-    def launch(part, step):
-        each, both = steps[step]
-        bit = orders[part][step]
-        high = bit_of(bit)
-        base = bases[part]
-        where = (flipped(bit), grp)
-        pending[part] = send(
-            piece(part, base + (1 - high) * each, each + both),
-            step_recv.at[part, step, pl.ds(0, (each + both) * SUBLANES)],
-            where,
-        )
-        history[part].append((where, base, base + high * (each + both), each))
-        bases[part] = base + high * each
-
-    def launch_grp(part):
-        base = bases[part]
-        for step in range(1, m):
-            peer = lax.rem(grp + step, m)
-            if grp_each:
-                copy = send(
-                    piece(part, base + peer * grp_each, grp_each),
-                    grp_recv.at[part, step - 1, pl.ds(0, grp_each * SUBLANES)],
-                    (blk, peer),
-                )
-                grp_copies[part].append(copy)
-            if grp_both:
-                copy = send(
-                    piece(part, base + m * grp_each, grp_both),
-                    grp_recv.at[
-                        part, step - 1, pl.ds(grp_each * SUBLANES, grp_both * SUBLANES)
-                    ],
-                    (blk, peer),
-                )
-                grp_copies[part].append(copy)
-
-    def advance(part, step):
-        if step < len(steps):
-            launch(part, step)
-        else:
-            launch_grp(part)
-
-    for part in range(2):
-        first_copies[part].wait_recv()
-        grads[mine, part] += first_recv[part]
-        advance(part, 0)
+    for unit in units:
+        next(unit)
     new_target, new_target_sums = target_step()
     target_out[0] = new_target
     target_state_out[...] = new_target_sums
-    for step in range(len(steps)):
-        each, both = steps[step]
-        for part in range(2):
-            pending[part].wait_recv()
-            if both:
-                pending[part].wait_send()
-                sent.append(id(pending[part]))
-            where = span(bases[part], each + both)
-            grads[mine, part, where] += step_recv[part, step, : (each + both) * SUBLANES]
-            advance(part, step + 1)
-
-    def summed(part, base, first, tiles):
-        own = grads[mine, part, span(base, tiles)]
-        total = None
-        for member in range(m):
-            slot = lax.max(lax.rem(grp - member + m, m) - 1, 0)
-            came = grp_recv[part, slot, first * SUBLANES : (first + tiles) * SUBLANES]
-            term = jnp.where(grp == member, own, came)
-            total = term if total is None else total + term
-        result[mine, part, span(base, tiles)] = total
-
-    out_pending = [[], []]
-    for part in range(2):
-        for copy in grp_copies[part]:
-            copy.wait_recv()
-        base = bases[part]
-        if grp_both:
-            summed(part, base + m * grp_each, grp_each, grp_both)
-        if grp_each:
-            summed(part, base + grp * grp_each, 0, grp_each)
-            for step in range(1, m):
-                ref = result.at[mine, part, span(base + grp * grp_each, grp_each)]
-                out_pending[part].append(send(ref, ref, (blk, lax.rem(grp + step, m))))
-    for back in range(len(steps) - 1, -1, -1):
-        for part in range(2):
-            where, base, first, each = history[part][back]
-            for copy in out_pending[part]:
-                copy.wait_recv()
-            out_pending[part] = []
-            if each:
-                ref = result.at[mine, part, span(first, each)]
-                out_pending[part] = [send(ref, ref, where)]
-    for part in range(2):
-        for copy in out_pending[part]:
-            copy.wait_recv()
-        ref = result.at[mine, part]
-        out_pending[part] = [send(ref, ref, core)]
-    for part in range(2):
-        out_pending[part][0].wait_recv()
+    while units:
+        units = [unit for unit in units if next(unit, done) is not done]
     for side in range(2):
         for part in range(2):
             lanes = slice((2 * side + part) * quarter, (2 * side + part + 1) * quarter)
@@ -335,6 +366,17 @@
             copy.wait_send()
 
 
+def store(*refs):
+    copies = [
+        pltpu.make_async_copy(refs[number], refs[6 + number], refs[12].at[number])
+        for number in range(6)
+    ]
+    for copy in copies:
+        copy.start()
+    for copy in copies:
+        copy.wait()
+
+
 def on_device(n, m, *arrays):
     arrays = list(arrays)
     rounds, slots = arrays[6].shape[0], arrays[6].shape[3]
@@ -346,34 +388,50 @@
     arrays[5] = arrays[5].reshape(1, kinds)
     arrays[9] = jnp.transpose(arrays[9], (1, 2, 0))
     quarter = kinds // 4
-    steps, (grp_each, grp_both) = plan(n, m, width)
+    chunks = chunks_of(width)
+    plans = [plan(n, m, tiles) for _, tiles in chunks]
     copies = copy_count(n, m, width, rounds)
-    largest = SUBLANES * sum(steps[0])
+    largest = SUBLANES * max(sum(steps[0]) for steps, _ in plans)
+    spread = SUBLANES * max(sum(last) for _, last in plans)
     slab = (max(rounds - 1, 1), width + SUBLANES, rows)
     vmem = pl.BlockSpec(memory_space=pltpu.VMEM)
-    smem = pl.BlockSpec(memory_space=pltpu.SMEM)
+    hbm = pl.BlockSpec(memory_space=pltpu.HBM)
+    staged = [pltpu.VMEM(a.shape, a.dtype) for a in arrays]
+    staged[9] = pltpu.SMEM(arrays[9].shape, arrays[9].dtype)
+    shapes = [jax.ShapeDtypeStruct(a.shape, F32) for a in arrays[:6]]
+    arrays = [pltpu.with_memory_space_constraint(a, pltpu.HBM) for a in arrays]
     outs = pl.pallas_call(
         functools.partial(kernel, n, m),
-        out_shape=[jax.ShapeDtypeStruct(a.shape, F32) for a in arrays[:6]],
-        in_specs=[vmem] * 9 + [smem, vmem],
+        out_shape=shapes,
+        in_specs=[hbm] * 11,
         out_specs=[vmem] * 6,
-        scratch_shapes=[
+        scratch_shapes=staged
+        + [
             pltpu.VMEM((rounds, kinds, slots), BF16),
             pltpu.VMEM((2, 2, width, quarter), F32),
             pltpu.VMEM((2, 2, width, quarter), F32),
             pltpu.VMEM(slab, F32),
             pltpu.VMEM(slab, F32),
             pltpu.VMEM((2, width, quarter), F32),
-            pltpu.VMEM((2, len(steps), largest, quarter), F32),
-            pltpu.VMEM((2, m - 1, (grp_each + grp_both) * SUBLANES, quarter), F32),
+            pltpu.VMEM((len(chunks), 2, len(plans[0][0]), largest, quarter), F32),
+            pltpu.VMEM((len(chunks), 2, m - 1, spread, quarter), F32),
             pltpu.SemaphoreType.DMA((copies,)),
             pltpu.SemaphoreType.DMA((copies,)),
+            pltpu.SemaphoreType.DMA((11,)),
         ],
         compiler_params=pltpu.CompilerParams(
             collective_id=0, has_side_effects=True, vmem_limit_bytes=40 * 2**20
         ),
         name="train",
     )(*arrays)
+    outs = pl.pallas_call(
+        store,
+        out_shape=shapes,
+        in_specs=[vmem] * 6,
+        out_specs=[hbm] * 6,
+        scratch_shapes=[pltpu.SemaphoreType.DMA((6,))],
+        name="store",
+    )(*outs)
     return (
         jnp.swapaxes(outs[0], 1, 2),
         outs[1],

time: 51.1 us -> 45.1 us (0.88)
  local copies, waits for them, and re-layouts: 10.2 us -> 3.87 us
    unnamed x28 -> x12, local copies, waits for them, and re-layouts: 10.2 us -> 3.87 us
    pallas_call x1 -> x2, Pallas kernels: 39.9 us -> 40.4 us  [the longest x1 38 us: on_device(): pl.pallas_call(functools.partial(kernel, n, m), out_shape=shapes, in_spec...]
where the time goes in v2:
time: 45.1 us; the launch traced here: 45 us
  Pallas kernels  40.4 us (90%)
  local copies, waits for them, and re-layouts  3.87 us (9%)
  between operations  0.66 us (1%)
    pallas_call x1, Pallas kernels, on_device(): pl.pallas_call(functools.partial(kernel, n, m), out_shape=shapes, in_spec...  38 us
    unnamed x12, local copies, waits for them, and re-layouts  3.87 us
    pallas_call x1, Pallas kernels, on_device(): pl.pallas_call(store, out_shape=shapes, in_specs=[vmem] * 6, out_specs=[h...  2.45 us

profile of v2, /device:TPU:1, one launch (start us, length us, event | category | flops | bytes accessed | tf_op | source)
XLA Modules:
  0.0 45.0 jit_solution(13626801350482355488)
XLA Ops:
  0.6 38.0 %train.1 = (f32[1,400,128]{2,1,0:T(8,128)S(1)}, f32[1,128]{1,0:T(1,128)S(1)}, f32[1,400,128]{2,1,0:T(8,128)S(1)}, f32[1,128]{1,0:T(1,128)S(1)}, f32[400,512]{1,0:T(8,128)S(1)}, /*index=5*/f32[1,512]{1,0:T(1,128)S(1)}) custom-call(f32[1,400,128]{2,1,0:T(8,128)} %bitcast.10, f32[1,128]{1,0:T(1,128)} %refs_1_.1, f32[1,400,128]{2,1,0:T(8,128)} %bitcast.11, ...), custom_call_target="tpu_custom_call" | custom-call | tf_op jit(solution)/shard_map/train/pallas_call | solution.py:403
  38.6 0.0 copy-start
  38.6 0.9 %copy-done = f32[400,512]{1,0:T(8,128)} copy-done((f32[400,512]{1,0:T(8,128)}, f32[400,512]{1,0:T(8,128)S(1)}, u32[]{:S(2)}) %copy-start) | copy-done | bytes 819224
  39.5 0.0 copy-start.1
  39.5 0.7 %copy-done.1 = f32[1,400,128]{2,1,0:T(8,128)} copy-done((f32[1,400,128]{2,1,0:T(8,128)}, f32[1,400,128]{2,1,0:T(8,128)S(1)}, u32[]{:S(2)}) %copy-start.1) | copy-done | bytes 204824
  40.2 0.0 copy-start.2
  40.2 0.7 %copy-done.2 = f32[1,400,128]{2,1,0:T(8,128)} copy-done((f32[1,400,128]{2,1,0:T(8,128)}, f32[1,400,128]{2,1,0:T(8,128)S(1)}, u32[]{:S(2)}) %copy-start.2) | copy-done | bytes 204824
  40.9 0.0 copy-start.4
  40.9 0.6 %copy-done.4 = f32[1,128]{1,0:T(1,128)} copy-done((f32[1,128]{1,0:T(1,128)}, f32[1,128]{1,0:T(1,128)S(1)}, u32[]{:S(2)}) %copy-start.4) | copy-done | bytes 536
  41.5 0.0 copy-start.5
  41.5 0.5 %copy-done.5 = f32[1,128]{1,0:T(1,128)} copy-done((f32[1,128]{1,0:T(1,128)}, f32[1,128]{1,0:T(1,128)S(1)}, u32[]{:S(2)}) %copy-start.5) | copy-done | bytes 536
  41.9 0.0 copy-start.3
  41.9 0.6 %copy-done.3 = f32[1,512]{1,0:T(1,128)} copy-done((f32[1,512]{1,0:T(1,128)}, f32[1,512]{1,0:T(1,128)S(1)}, u32[]{:S(2)}) %copy-start.3) | copy-done | bytes 2072
  42.5 2.5 %store.1 = (f32[1,400,128]{2,1,0:T(8,128)}, f32[1,128]{1,0:T(1,128)}, f32[1,400,128]{2,1,0:T(8,128)}, f32[1,128]{1,0:T(1,128)}, f32[400,512]{1,0:T(8,128)}, /*index=5*/f32[1,512]{1,0:T(1,128)}) custom-call(f32[1,400,128]{2,1,0:T(8,128)} %copy-done.1, f32[1,128]{1,0:T(1,128)} %copy-done.4, f32[1,400,128]{2,1,0:T(8,128)} %copy-done.2, f32[1,128]{1,0:T(1,128)} %copy-done.5, ...), custom_call_target="tpu_custom_call" | custom-call | tf_op jit(solution)/shard_map/store/pallas_call | solution.py:427
Async XLA Ops:
  38.6 0.9 %copy-start = (f32[400,512]{1,0:T(8,128)}, f32[400,512]{1,0:T(8,128)S(1)}, u32[]{:S(2)}) copy-start(f32[400,512]{1,0:T(8,128)S(1)} %get-tuple-element.22.refs_4_) | copy-start | bytes 2457604
  39.5 0.7 %copy-start.1 = (f32[1,400,128]{2,1,0:T(8,128)}, f32[1,400,128]{2,1,0:T(8,128)S(1)}, u32[]{:S(2)}) copy-start(f32[1,400,128]{2,1,0:T(8,128)S(1)} %get-tuple-element.18.refs_0_) | copy-start | bytes 614404
  40.2 0.7 %copy-start.2 = (f32[1,400,128]{2,1,0:T(8,128)}, f32[1,400,128]{2,1,0:T(8,128)S(1)}, u32[]{:S(2)}) copy-start(f32[1,400,128]{2,1,0:T(8,128)S(1)} %get-tuple-element.20.refs_2_) | copy-start | bytes 614404
  40.9 0.6 %copy-start.4 = (f32[1,128]{1,0:T(1,128)}, f32[1,128]{1,0:T(1,128)S(1)}, u32[]{:S(2)}) copy-start(f32[1,128]{1,0:T(1,128)S(1)} %get-tuple-element.19.refs_1_) | copy-start | bytes 1540
  41.5 0.5 %copy-start.5 = (f32[1,128]{1,0:T(1,128)}, f32[1,128]{1,0:T(1,128)S(1)}, u32[]{:S(2)}) copy-start(f32[1,128]{1,0:T(1,128)S(1)} %get-tuple-element.21.refs_3_) | copy-start | bytes 1540
  41.9 0.6 %copy-start.3 = (f32[1,512]{1,0:T(1,128)}, f32[1,512]{1,0:T(1,128)S(1)}, u32[]{:S(2)}) copy-start(f32[1,512]{1,0:T(1,128)S(1)} %get-tuple-element.23.refs_5_) | copy-start | bytes 6148

commit v3 on v2

--- a/solution.py
+++ b/solution.py
@@ -12,7 +12,6 @@
 MESH = pl.DeviceIdType.MESH
 BF16 = jnp.bfloat16
 F32 = jnp.float32
-done = object()
 
 
 def halves_of(x):
@@ -188,21 +187,24 @@
     for index in range(rounds):
         source_hot, target_hot, share, alive = edges
         source_high, source_low = halves_of(source)
-        left = mm(source_high, source_hot) + mm(source_low, source_hot)
+        left = mm(
+            jnp.concatenate([source_high, source_low], axis=1),
+            jnp.concatenate([source_hot, source_hot], axis=0),
+        )
         query = left * scale
         query_high, query_low = halves_of(query)
         flat_high, flat_low = halves_of(target.T)
-        logits = mm(flat_high, query_high) + (
-            mm(flat_low, query_high) + mm(flat_high, query_low)
-        )
+        both = mm(jnp.concatenate([flat_high, flat_low], axis=0), query_high)
+        logits = both[:rows] + (both[rows:] + mm(flat_high, query_low))
         positive = jnp.sum(jnp.where(target_hot, logits, 0.0), axis=0, keepdims=True)
         pull = -alive * jax.nn.sigmoid(-positive)
         push = share * alive * jax.nn.sigmoid(logits)
         weight = jnp.where(target_hot, pull, 0.0) + push
         weight_high, weight_low = halves_of(weight)
         target_high, target_low = halves_of(target)
-        grad_query = mm(target_high, weight_high) + (
-            mm(target_low, weight_high) + mm(target_high, weight_low)
+        grad_query = mm(
+            jnp.concatenate([target_high, target_low, target_high], axis=1),
+            jnp.concatenate([weight_high, weight_high, weight_low], axis=0),
         )
 
         def source_step():
@@ -211,9 +213,8 @@
             return adagrad(source, source_sums, fresh)
 
         def target_step():
-            fresh = mm_nt(query_high, weight_high) + (
-                mm_nt(query_high, weight_low) + mm_nt(query_low, weight_high)
-            )
+            pair = mm_nt(query_high, jnp.concatenate([weight_high, weight_low], axis=0))
+            fresh = pair[:, :rows] + (pair[:, rows:] + mm_nt(query_low, weight_high))
             return adagrad(target, target_sums, fresh)
 
         relation_high, relation_low = halves_of(grad_query * left)
@@ -351,16 +352,24 @@
     new_target, new_target_sums = target_step()
     target_out[0] = new_target
     target_state_out[...] = new_target_sums
-    while units:
-        units = [unit for unit in units if next(unit, done) is not done]
-    for side in range(2):
-        for part in range(2):
-            lanes = slice((2 * side + part) * quarter, (2 * side + part + 1) * quarter)
-            fresh, sums = adagrad(
-                relation_ref[:, lanes], relation_state_ref[:, lanes], result[side, part]
-            )
-            relation_out[:, lanes] = fresh
-            relation_state_out[:, lanes] = sums
+    for _ in range(2 * (bits - 1) + 2):
+        for unit in units:
+            next(unit)
+
+    def relation_step(side, part):
+        lanes = pl.ds(pl.multiple_of((2 * side + part) * quarter, quarter), quarter)
+        fresh, sums = adagrad(
+            relation_ref[:, lanes], relation_state_ref[:, lanes], result[side, part]
+        )
+        relation_out[:, lanes] = fresh
+        relation_state_out[:, lanes] = sums
+
+    for part in range(2):
+        relation_step(mine, part)
+    for unit in units:
+        next(unit, None)
+    for part in range(2):
+        relation_step(1 - mine, part)
     for copy in started:
         if id(copy) not in sent:
             copy.wait_send()
@@ -402,7 +411,7 @@
     arrays = [pltpu.with_memory_space_constraint(a, pltpu.HBM) for a in arrays]
     outs = pl.pallas_call(
         functools.partial(kernel, n, m),
-        out_shape=shapes,
+        out_shape=[pltpu.VMEM(a.shape, F32) for a in arrays[:6]],
         in_specs=[hbm] * 11,
         out_specs=[vmem] * 6,
         scratch_shapes=staged
@@ -424,6 +433,7 @@
         ),
         name="train",
     )(*arrays)
+    outs = [pltpu.with_memory_space_constraint(a, pltpu.VMEM) for a in outs]
     outs = pl.pallas_call(
         store,
         out_shape=shapes,

time: 45.1 us -> 39 us (0.86)
  local copies, waits for them, and re-layouts: 3.87 us -> 0 us
  Pallas kernels: 40.4 us -> 38.3 us
    unnamed x12 -> x0, local copies, waits for them, and re-layouts: 3.87 us -> none
    pallas_call x1, Pallas kernels: 2.45 us -> 1.09 us  [on_device(): pl.pallas_call(store, out_shape=shapes, in_specs=[vmem] * 6, out_specs=[h...]
    pallas_call x1, Pallas kernels: 38 us -> 37.2 us  [on_device(): pl.pallas_call(functools.partial(kernel, n, m), out_shape=[pltpu.VMEM(a.s...]
where the time goes in v3:
time: 39 us; the launch traced here: 38.9 us
  Pallas kernels  38.3 us (98%)
  between operations  0.64 us (2%)
    pallas_call x1, Pallas kernels, on_device(): pl.pallas_call(functools.partial(kernel, n, m), out_shape=[pltpu.VMEM(a.s...  37.2 us
    pallas_call x1, Pallas kernels, on_device(): pl.pallas_call(store, out_shape=shapes, in_specs=[vmem] * 6, out_specs=[h...  1.09 us

profile of v3, /device:TPU:1, one launch (start us, length us, event | category | flops | bytes accessed | tf_op | source)
XLA Modules:
  0.0 38.9 jit_solution(13140181673004749302)
XLA Ops:
  0.6 37.2 %train.1 = (f32[1,400,128]{2,1,0:T(8,128)S(1)}, f32[1,128]{1,0:T(1,128)S(1)}, f32[1,400,128]{2,1,0:T(8,128)S(1)}, f32[1,128]{1,0:T(1,128)S(1)}, f32[400,512]{1,0:T(8,128)S(1)}, /*index=5*/f32[1,512]{1,0:T(1,128)S(1)}) custom-call(f32[1,400,128]{2,1,0:T(8,128)} %bitcast.10, f32[1,128]{1,0:T(1,128)} %refs_1_.1, f32[1,400,128]{2,1,0:T(8,128)} %bitcast.11, ...), custom_call_target="tpu_custom_call" | custom-call | tf_op jit(solution)/shard_map/train/pallas_call | solution.py:412
  37.8 1.1 %store.1 = (f32[1,400,128]{2,1,0:T(8,128)}, f32[1,128]{1,0:T(1,128)}, f32[1,400,128]{2,1,0:T(8,128)}, f32[1,128]{1,0:T(1,128)}, f32[400,512]{1,0:T(8,128)}, /*index=5*/f32[1,512]{1,0:T(1,128)}) custom-call(f32[1,400,128]{2,1,0:T(8,128)S(1)} %get-tuple-element.18.refs_0_, f32[1,128]{1,0:T(1,128)S(1)} %get-tuple-element.19.refs_1_, ...), custom_call_target="tpu_custom_call" | custom-call | tf_op jit(solution)/shard_map/store/pallas_call | solution.py:437

commit v4 on v3

--- a/solution.py
+++ b/solution.py
@@ -34,8 +34,10 @@
 
 def chunks_of(width):
     tiles = width // SUBLANES
-    large = 1 << (tiles.bit_length() - 1)
-    return [(0, large), (large, tiles - large)] if large < tiles else [(0, tiles)]
+    usual = max((1 << (tiles.bit_length() - 1)) // 2, 1)
+    sizes = [usual] * (tiles // usual)
+    sizes[0] += tiles % usual
+    return [(sum(sizes[:number]), size) for number, size in enumerate(sizes)]
 
 
 def plan(n, m, tiles):
@@ -114,7 +116,7 @@
         pltpu.make_async_copy(src, dst, load_sem.at[number])
         for number, (src, dst) in enumerate(zip(hbm, staged))
     ]
-    for number in (4, 8, 0, 6, 2, 7, 10, 9, 1, 3, 5):
+    for number in (8, 4, 6, 7, 10, 9, 0, 2, 1, 3, 5):
         loads[number].start()
     blk, grp = lax.axis_index("blk"), lax.axis_index("grp")
     bits = n.bit_length() - 1
@@ -154,14 +156,17 @@
         started.append(copy)
         return copy
 
-    loads[4].wait()
-    table_high, table_low = halves_of(relation_ref[...])
-
-    def relation_side(index):
+    def kinds_of(index):
         picked = relation_ids_ref[index, 0]
         hot = (lax.broadcasted_iota(jnp.int32, (kinds, slots), 0) == picked).astype(BF16)
         hot_ref[index] = hot
+        return hot
+
+    def scale_of(hot):
         return mm(table_high, hot) + mm(table_low, hot)
+
+    def target_side(target):
+        return halves_of(target), halves_of(target.T)
 
     def edge_side(index):
         row_iota = lax.broadcasted_iota(jnp.int32, (rows, slots), 0)
@@ -176,12 +181,18 @@
         return source_hot, target_hot, share, alive
 
     loads[8].wait()
-    scale = relation_side(0)
-    for number in (0, 6, 2, 7, 10, 9, 1, 3, 5):
+    hot = kinds_of(0)
+    for number in (6, 7, 10, 9):
+        loads[number].wait()
+    edges = edge_side(0)
+    loads[4].wait()
+    table_high, table_low = halves_of(relation_ref[...])
+    scale = scale_of(hot)
+    for number in (0, 2, 1, 3, 5):
         loads[number].wait()
     source, source_sums = source_ref[0], source_state_ref[...]
     target, target_sums = target_ref[0], target_state_ref[...]
-    edges = edge_side(0)
+    sides = target_side(target)
     pl.semaphore_wait(barrier, len(greeted))
 
     for index in range(rounds):
@@ -193,7 +204,7 @@
         )
         query = left * scale
         query_high, query_low = halves_of(query)
-        flat_high, flat_low = halves_of(target.T)
+        (target_high, target_low), (flat_high, flat_low) = sides
         both = mm(jnp.concatenate([flat_high, flat_low], axis=0), query_high)
         logits = both[:rows] + (both[rows:] + mm(flat_high, query_low))
         positive = jnp.sum(jnp.where(target_hot, logits, 0.0), axis=0, keepdims=True)
@@ -201,7 +212,6 @@
         push = share * alive * jax.nn.sigmoid(logits)
         weight = jnp.where(target_hot, pull, 0.0) + push
         weight_high, weight_low = halves_of(weight)
-        target_high, target_low = halves_of(target)
         grad_query = mm(
             jnp.concatenate([target_high, target_low, target_high], axis=1),
             jnp.concatenate([weight_high, weight_high, weight_low], axis=0),
@@ -237,9 +247,10 @@
             new_target, new_target_sums = target_step()
             relation_part(0)
             relation_part(1)
-            scale = relation_side(index + 1)
+            scale = scale_of(kinds_of(index + 1))
             edges = edge_side(index + 1)
             target, target_sums = new_target, new_target_sums
+            sides = target_side(target)
             copy.wait_recv()
             source = slab_recv[index, :width]
             source_sums = slab_recv[index, width : width + 1]
@@ -344,6 +355,8 @@
     for unit in units:
         next(unit)
     relation_part(mine)
+    for unit in units:
+        next(unit)
     new_source, new_sums = source_step()
     source_out[0] = new_source
     source_state_out[...] = new_sums
@@ -352,7 +365,7 @@
     new_target, new_target_sums = target_step()
     target_out[0] = new_target
     target_state_out[...] = new_target_sums
-    for _ in range(2 * (bits - 1) + 2):
+    for _ in range(2 * (bits - 1) + 1):
         for unit in units:
             next(unit)
 

time: 39 us -> 39.1 us (level)
  no operation moved by 1% of the time
where the time goes in v4:
time: 39.1 us; the launch traced here: 38.9 us
  Pallas kernels  38.2 us (98%)
  between operations  0.64 us (2%)
    pallas_call x1, Pallas kernels, on_device(): pl.pallas_call(functools.partial(kernel, n, m), out_shape=[pltpu.VMEM(a.s...  37.1 us
    pallas_call x1, Pallas kernels, on_device(): pl.pallas_call(store, out_shape=shapes, in_specs=[vmem] * 6, out_specs=[h...  1.09 us

profile of v4, /device:TPU:1, one launch (start us, length us, event | category | flops | bytes accessed | tf_op | source)
XLA Modules:
  0.0 38.9 jit_solution(7351490130855260054)
XLA Ops:
  0.6 37.1 %train.1 = (f32[1,400,128]{2,1,0:T(8,128)S(1)}, f32[1,128]{1,0:T(1,128)S(1)}, f32[1,400,128]{2,1,0:T(8,128)S(1)}, f32[1,128]{1,0:T(1,128)S(1)}, f32[400,512]{1,0:T(8,128)S(1)}, /*index=5*/f32[1,512]{1,0:T(1,128)S(1)}) custom-call(f32[1,400,128]{2,1,0:T(8,128)} %bitcast.10, f32[1,128]{1,0:T(1,128)} %refs_1_.1, f32[1,400,128]{2,1,0:T(8,128)} %bitcast.11, ...), custom_call_target="tpu_custom_call" | custom-call | tf_op jit(solution)/shard_map/train/pallas_call | solution.py:425
  37.8 1.1 %store.1 = (f32[1,400,128]{2,1,0:T(8,128)}, f32[1,128]{1,0:T(1,128)}, f32[1,400,128]{2,1,0:T(8,128)}, f32[1,128]{1,0:T(1,128)}, f32[400,512]{1,0:T(8,128)}, /*index=5*/f32[1,512]{1,0:T(1,128)}) custom-call(f32[1,400,128]{2,1,0:T(8,128)S(1)} %get-tuple-element.18.refs_0_, f32[1,128]{1,0:T(1,128)S(1)} %get-tuple-element.19.refs_1_, ...), custom_call_target="tpu_custom_call" | custom-call | tf_op jit(solution)/shard_map/store/pallas_call | solution.py:450

commit v5 on v4

--- a/solution.py
+++ b/solution.py
@@ -163,7 +163,8 @@
         return hot
 
     def scale_of(hot):
-        return mm(table_high, hot) + mm(table_low, hot)
+        pair = mm(table_pair, hot)
+        return pair[:width] + pair[width:]
 
     def target_side(target):
         return halves_of(target), halves_of(target.T)
@@ -186,7 +187,7 @@
         loads[number].wait()
     edges = edge_side(0)
     loads[4].wait()
-    table_high, table_low = halves_of(relation_ref[...])
+    table_pair = jnp.concatenate(halves_of(relation_ref[...]), axis=0)
     scale = scale_of(hot)
     for number in (0, 2, 1, 3, 5):
         loads[number].wait()
@@ -218,8 +219,9 @@
         )
 
         def source_step():
-            high, low = halves_of(grad_query * scale)
-            fresh = mm_nt(high, source_hot) + mm_nt(low, source_hot)
+            pair = jnp.concatenate(halves_of(grad_query * scale), axis=0)
+            pair = mm_nt(pair, source_hot)
+            fresh = pair[:width] + pair[width:]
             return adagrad(source, source_sums, fresh)
 
         def target_step():
@@ -227,11 +229,12 @@
             fresh = pair[:, :rows] + (pair[:, rows:] + mm_nt(query_low, weight_high))
             return adagrad(target, target_sums, fresh)
 
-        relation_high, relation_low = halves_of(grad_query * left)
+        relation_pair = jnp.concatenate(halves_of(grad_query * left), axis=0)
 
         def relation_part(core):
             hot = hot_ref[index, pl.ds(pl.multiple_of(core * 2 * quarter, quarter), 2 * quarter)]
-            fresh = mm_nt(relation_high, hot) + mm_nt(relation_low, hot)
+            pair = mm_nt(relation_pair, hot)
+            fresh = pair[:width] + pair[width:]
             for part in range(2):
                 piece = fresh[:, part * quarter : (part + 1) * quarter]
                 if index == 0:

time: 39.1 us -> 39 us (level)
  no operation moved by 1% of the time
where the time goes in v5:
time: 39 us; the launch traced here: 38.9 us
  Pallas kernels  38.2 us (98%)
  between operations  0.64 us (2%)
    pallas_call x1, Pallas kernels, on_device(): pl.pallas_call(functools.partial(kernel, n, m), out_shape=[pltpu.VMEM(a.s...  37.1 us
    pallas_call x1, Pallas kernels, on_device(): pl.pallas_call(store, out_shape=shapes, in_specs=[vmem] * 6, out_specs=[h...  1.09 us

profile of v5, /device:TPU:1, one launch (start us, length us, event | category | flops | bytes accessed | tf_op | source)
XLA Modules:
  0.0 38.9 jit_solution(6820316186892734051)
XLA Ops:
  0.6 37.1 %train.1 = (f32[1,400,128]{2,1,0:T(8,128)S(1)}, f32[1,128]{1,0:T(1,128)S(1)}, f32[1,400,128]{2,1,0:T(8,128)S(1)}, f32[1,128]{1,0:T(1,128)S(1)}, f32[400,512]{1,0:T(8,128)S(1)}, /*index=5*/f32[1,512]{1,0:T(1,128)S(1)}) custom-call(f32[1,400,128]{2,1,0:T(8,128)} %bitcast.10, f32[1,128]{1,0:T(1,128)} %refs_1_.1, f32[1,400,128]{2,1,0:T(8,128)} %bitcast.11, ...), custom_call_target="tpu_custom_call" | custom-call | tf_op jit(solution)/shard_map/train/pallas_call | solution.py:428
  37.8 1.1 %store.1 = (f32[1,400,128]{2,1,0:T(8,128)}, f32[1,128]{1,0:T(1,128)}, f32[1,400,128]{2,1,0:T(8,128)}, f32[1,128]{1,0:T(1,128)}, f32[400,512]{1,0:T(8,128)}, /*index=5*/f32[1,512]{1,0:T(1,128)}) custom-call(f32[1,400,128]{2,1,0:T(8,128)S(1)} %get-tuple-element.18.refs_0_, f32[1,128]{1,0:T(1,128)S(1)} %get-tuple-element.19.refs_1_, ...), custom_call_target="tpu_custom_call" | custom-call | tf_op jit(solution)/shard_map/store/pallas_call | solution.py:453
